TPU v7x, 32 devices: a whole 2x2x4 slice. The times are simulated.
32 devices in a mesh: dp: 4 (over y, x), fsdp: 8 (over z, core).
Axes of the slice: x: 2, y: 2, z: 4, core: 2. Of those that a mesh axis runs over, the one named last changes fastest.
Arguments:
- stream_in: bfloat16 [65536, 512], P(('dp', 'fsdp')), may hold values from -6 to 6
- dual_in: float32 [65536, 512], P(('dp', 'fsdp')), may hold values from -6 to 6
- segment_ids: int32 [64, 1024], P(('dp', 'fsdp')), may hold values from 0 to 8, as said below
- qkv_weight: float32 [512, 1536], P(('dp', 'fsdp')), may hold values from -0.25 to 0.25
- proj_weight: float32 [512, 512], P(('dp', 'fsdp')), may hold values from -1 to 1
- up_weight: float32 [512, 2048], P(('dp', 'fsdp')), may hold values from -0.25 to 0.25
- down_weight: float32 [2048, 512], P(('dp', 'fsdp')), may hold values from -0.1875 to 0.1875
- vectors: float32 [6144], P(('dp', 'fsdp')), may hold values from -1.2 to 2.2
- qkv_first: float32 [512, 1536], P(('dp', 'fsdp')), may hold values from -768 to 768
- proj_first: float32 [512, 512], P(('dp', 'fsdp')), may hold values from -320 to 320
- up_first: float32 [512, 2048], P(('dp', 'fsdp')), may hold values from -640 to 640
- down_first: float32 [2048, 512], P(('dp', 'fsdp')), may hold values from -1280 to 1280
- vec_first: float32 [6144], P(('dp', 'fsdp')), may hold values from -1024 to 1024
- qkv_second: float32 [512, 1536], P(('dp', 'fsdp')), may hold values from 16384 to 65536
- proj_second: float32 [512, 512], P(('dp', 'fsdp')), may hold values from 2621.44 to 10485.76
- up_second: float32 [512, 2048], P(('dp', 'fsdp')), may hold values from 10485.76 to 41943.04
- down_second: float32 [2048, 512], P(('dp', 'fsdp')), may hold values from 41943.04 to 167772.16
- vec_second: float32 [6144], P(('dp', 'fsdp')), may hold values from 6553.6 to 7864320
- cot_stream: bfloat16 [65536, 512], P(('dp', 'fsdp')), may hold values from -6 to 6
- cot_dual: bfloat16 [65536, 512], P(('dp', 'fsdp')), may hold values from -6 to 6
Outputs:
- stream_out: bfloat16 [65536, 512], P(('dp', 'fsdp'))
- dual_out: float32 [65536, 512], P(('dp', 'fsdp'))
- stream_grad: float32 [65536, 512], P(('dp', 'fsdp'))
- root_means: float32 [3], replicated
- qkv_grad: float32 [512, 1536], P(('dp', 'fsdp'))
- proj_grad: float32 [512, 512], P(('dp', 'fsdp'))
- up_grad: float32 [512, 2048], P(('dp', 'fsdp'))
- down_grad: float32 [2048, 512], P(('dp', 'fsdp'))
- vec_grad: float32 [6144], P(('dp', 'fsdp'))
- qkv_renewed: float32 [512, 1536], P(('dp', 'fsdp'))
- proj_renewed: float32 [512, 512], P(('dp', 'fsdp'))
- up_renewed: float32 [512, 2048], P(('dp', 'fsdp'))
- down_renewed: float32 [2048, 512], P(('dp', 'fsdp'))
- vec_renewed: float32 [6144], P(('dp', 'fsdp'))
- qkv_updated: float32 [512, 1536], P(('dp', 'fsdp'))
- proj_updated: float32 [512, 512], P(('dp', 'fsdp'))
- up_updated: float32 [512, 2048], P(('dp', 'fsdp'))
- down_updated: float32 [2048, 512], P(('dp', 'fsdp'))
- vec_updated: float32 [6144], P(('dp', 'fsdp'))
Inputs may be any that keep to these rules, and one draw needn't show every extreme that they name: `segment_ids`: in each row the nonzero ids start at 1 and never fall; padding (id 0) fills the row's tail; at least 256 positions of every row are nonzero; ids are at most min(8, 256), documents beyond that sharing the last number.
All inputs are finite; a program needn't handle non-finite values.
Results may differ from a plain program's by a relative error of at most 0.013.
The roundings to bfloat16 on the way count: a program that leaves them out, or rounds other values in their place, can miss the bound.
Values may be sent and summed in bfloat16 or wider, within the bound.
A program may use at most 256 MiB of HBM per device.

v0:
```python
import functools

import jax
import jax.numpy as jnp
from jax import lax
from jax.experimental import pallas as pl
from jax.experimental.pallas import tpu as pltpu
from jax.sharding import PartitionSpec as P

HEAD = 64
STEP = 10
NORM_EPS = 1e-05
BETA_FIRST = 0.5
BETA_SECOND = 0.5
ADAM_EPS = 1e-08
RATES = ((0.04, 0.1), (0.15, 0.1), (0.04, 0.1), (0.03, 0.1), (0.2, 0.0))

AXES = ("dp", "fsdp")
MESH = pl.DeviceIdType.MESH
bf16 = jnp.bfloat16
f32 = jnp.float32
ANY = pl.BlockSpec(memory_space=pl.ANY)
VMEM = pl.BlockSpec(memory_space=pltpu.VMEM)

SLOTS = 32
NEG = -1e30
QB = 256
LANES = 128


def nn(a, b):
    return jnp.dot(a, b, preferred_element_type=f32)


def nt(a, b):
    return lax.dot_general(a, b, (((1,), (1,)), ((), ())), preferred_element_type=f32)


def tn(a, b):
    return lax.dot_general(a, b, (((0,), (0,)), ((), ())), preferred_element_type=f32)


def merged(packed):
    return packed.reshape(-1, packed.shape[-1])


def half_rows():
    lane = lax.broadcasted_iota(jnp.int32, (1, LANES), 1)
    low = jnp.where(lane < HEAD, 1.0, 0.0)
    return low.astype(bf16), (1.0 - low).astype(bf16)


def segment_columns(seg_row):
    length = seg_row.shape[-1]
    place = lax.rem(lax.broadcasted_iota(jnp.int32, (LANES, length), 0), HEAD)
    ids = jnp.broadcast_to(seg_row, (LANES, length))
    same = (place == ids) & (place < 16)
    ones = jnp.where(same, 1.0, 0.0)
    against = jnp.where(place < 16, jnp.where(same, 0.0, NEG), jnp.where(place < 19, 1.0, 0.0))
    return jnp.transpose(ones).astype(bf16), jnp.transpose(against).astype(bf16)


def in_parts(value):
    first = value.astype(bf16).astype(f32)
    rest = value - first
    second = rest.astype(bf16).astype(f32)
    return first, second, rest - second


def part_columns(value, other):
    first, second, third = in_parts(value)
    lane = lax.rem(lax.broadcasted_iota(jnp.int32, value.shape, 1), HEAD)
    return jnp.where(
        lane == 16, first, jnp.where(lane == 17, second, jnp.where(lane == 18, third, other))
    )


class Place:
    def __init__(self):
        self.dp = lax.axis_index("dp")
        self.fs = lax.axis_index("fsdp")
        self.c = lax.rem(self.fs, 2)
        self.z = self.fs // 2
        x = lax.rem(self.dp, 2)
        y = self.dp // 2
        self.dpx = 2 * y + 1 - x
        self.dpy = 2 - 2 * y + x
        self.a = self.dpx + self.c * (self.dpy - self.dpx)
        self.b = self.dpy + self.c * (self.dpx - self.dpy)
        self.ab = 3 - self.dp
        self.zs = [lax.rem(self.z + k, 4) for k in range(4)]
        self.to_a = (self.a, self.fs)
        self.to_b = (self.b, self.fs)
        self.to_x = (self.dpx, self.fs)
        self.to_y = (self.dpy, self.fs)
        self.to_ab = (self.ab, self.fs)
        self.to_core = (self.dp, self.fs + 1 - 2 * self.c)
        self.to_z = [None] + [(self.dp, 2 * self.zs[k] + self.c) for k in range(1, 4)]

    def greet(self):
        friends = [self.to_a, self.to_b, self.to_ab, self.to_core] + self.to_z[1:]
        for friend in friends:
            pl.semaphore_signal(
                pltpu.get_barrier_semaphore(), inc=1, device_id=friend, device_id_type=MESH
            )

    def greeted(self):
        pl.semaphore_wait(pltpu.get_barrier_semaphore(), 7)


def remote(src, dst, send_sem, recv_sem, device):
    return pltpu.make_async_remote_copy(
        src_ref=src,
        dst_ref=dst,
        send_sem=send_sem,
        recv_sem=recv_sem,
        device_id=device,
        device_id_type=MESH,
    )


class Gather:
    def __init__(self, here, buf, columns, send_sem, recv_sem, straight):
        self.here, self.buf, self.columns = here, buf, columns
        self.send_sem, self.recv_sem, self.straight = send_sem, recv_sem, straight
        self.sent = []

    def slot_copy(self, number, z, device):
        slot = self.buf.at[self.here.dp, z, self.here.c, :, self.columns]
        return remote(slot, slot, self.send_sem.at[number], self.recv_sem.at[z], device)

    def line_copy(self, number, d, c, device):
        line = self.buf.at[d, :, c, :, self.columns]
        base = 4 if device is not self.here.to_core else 8
        return remote(line, line, self.send_sem.at[number], self.recv_sem.at[base + d], device)

    def send(self, d, *devices):
        for device in devices:
            number = 3 + len(self.sent)
            self.sent.append((d, device))
            self.line_copy(number, d, self.here.c, device).start()

    def arrive(self, d):
        self.line_copy(0, d, self.here.c, self.here.to_a).wait_recv()

    def step(self, number):
        me = self.here
        if number == 0:
            for k in range(1, 4):
                self.slot_copy(k - 1, me.z, me.to_z[k]).start()
        elif number == 1:
            for k in range(1, 4):
                self.slot_copy(0, me.zs[k], me.to_z[k]).wait_recv()
            if self.straight:
                self.send(me.dp, me.to_ab, me.to_a, me.to_b, me.to_core)
            else:
                self.send(me.dp, me.to_a, me.to_b, me.to_core)
        elif number == 2:
            self.arrive(me.a)
            self.send(me.a, *([me.to_core] if self.straight else [me.to_b, me.to_core]))
        elif number == 3:
            for d in (me.b, me.ab):
                self.arrive(d)
                self.send(d, me.to_core)
        else:
            for d in range(4):
                self.line_copy(0, d, 1 - me.c, me.to_core).wait_recv()

    def finish(self):
        me = self.here
        for k in range(1, 4):
            self.slot_copy(k - 1, me.z, me.to_z[k]).wait_send()
        for number, (d, device) in enumerate(self.sent):
            self.line_copy(3 + number, d, me.c, device).wait_send()


def forward_kernel(comm, scale, *refs):
    if comm:
        (x_hbm, seg, wqkv, wp, wu, wd, vec, qkv_o, mix_o, feat_o, vec_o, ga_o, gb_o, gc_o) = refs[:14]
        (x_v, now_v, next_v, mix_v, feat_v, fq, fk, ga, gb, gc) = refs[14:24]
        (loc, sa, ra, sb, rb, sc, rc) = refs[24:]
    else:
        (x_hbm, seg, ga_hbm, qkv_o, mix_o, feat_o, vec_o) = refs[:7]
        (x_v, now_v, next_v, mix_v, feat_v, fq, fk, ga) = refs[7:15]
        (loc,) = refs[15:]
    rows, length = seg.shape
    width = x_v.shape[1]
    pairs = width // LANES
    step_rows = width // SLOTS

    x_copy = pltpu.make_async_copy(x_hbm, x_v, loc.at[pairs, 0])
    count = SLOTS * 6
    if comm:
        here = Place()
        here.greet()
        own = (here.dp, here.z, here.c)
        for p in range(pairs):
            for j in range(3):
                begin = j * width + p * LANES
                ga[(p,) + own + (slice(None), slice(j * LANES, (j + 1) * LANES))] = wqkv[
                    :, begin : begin + LANES
                ].astype(bf16)
        rest = jnp.concatenate([vec[:, LANES:], jnp.zeros((1, 2 * LANES - count), f32)], axis=1)
        row = lax.broadcasted_iota(jnp.int32, (step_rows, LANES), 0)
        tile = jnp.where(row == 0, vec[:, :LANES], jnp.where(row == 1, rest, 0.0))
        ga[(0,) + own + (slice(None), slice(3 * LANES, 4 * LANES))] = tile.astype(bf16)
        gathers = [
            Gather(here, ga.at[p], slice(0, 4 * LANES if p == 0 else 3 * LANES), sa.at[p], ra.at[p], True)
            for p in range(pairs)
        ]
        every = slice(0, width)
        gathers.append(Gather(here, gb, every, sb, rb, False))
        gathers.append(Gather(here, gc, every, sc, rc, False))
        here.greeted()
        gathers[0].step(0)
        x_copy.start()
        for p in range(1, pairs):
            gathers[p].step(0)
        gb[own + (slice(0, step_rows),)] = wp[...].astype(bf16)
        for j in range(4):
            gb[own + (slice((j + 1) * step_rows, (j + 2) * step_rows),)] = wu[
                :, j * width : (j + 1) * width
            ].astype(bf16)
        gc[own] = wd[...].astype(bf16)
    else:
        x_copy.start()
        ga_copy = pltpu.make_async_copy(ga_hbm, ga, loc.at[pairs, 1])
        ga_copy.start()

    def marks_of(r):
        ones, against = segment_columns(seg[r : r + 1, :])
        fq[r] = ones
        fk[r] = against

    def transfer(*steps):
        for group, number in steps:
            gathers[group].step(number)

    if comm:
        transfer((0, 1), (4, 0), (1, 1))
        marks_of(0)
        transfer((0, 2), (0, 3), (2, 1), (5, 0))
        for r in range(1, rows):
            marks_of(r)
        transfer((0, 4))
    else:
        for r in range(rows):
            marks_of(r)
        ga_copy.wait()
    x_copy.wait()

    lane = lax.broadcasted_iota(jnp.int32, (1, LANES), 1)

    def half_of(number, upper):
        part = number % 3
        row = part // 2
        i = number // 3
        tile = ga[0, i // 8, i % 8 // 2, i % 2, :, 3 * LANES : 4 * LANES].astype(f32)
        tile = tile if upper == (part == 1) else pltpu.roll(tile, HEAD, 1)
        return tile[row : row + 1, :]

    def assemble(first, last):
        for t in range(first, last):
            line = jnp.where(lane < HEAD, half_of(2 * t, False), half_of(2 * t + 1, True))
            vec_o[t // 4 : t // 4 + 1, t % 4 * LANES : (t % 4 + 1) * LANES] = line

    assemble(4 * pairs, 6 * pairs)

    def columns_at(p):
        return pl.ds(pl.multiple_of(p * LANES, LANES), LANES)

    def project(p, part):
        lin = nn(x_v[part, :], merged(ga[p, :, :, :, :, : 3 * LANES]))
        query = (lin[:, :LANES] + vec_o[4:5, columns_at(p)]).astype(bf16).astype(f32) * scale
        next_v[0, part, :] = query.astype(bf16)
        next_v[1, part, :] = lin[:, LANES : 2 * LANES].astype(bf16)
        next_v[2, part, :] = (lin[:, 2 * LANES :] + vec_o[5:6, columns_at(p)]).astype(bf16)

    for t in range(rows * length // 512):
        project(0, slice(t * 512, (t + 1) * 512))
    if comm:
        transfer((1, 2), (1, 3))
    assemble(0, 4 * pairs)
    assemble(6 * pairs, 12 * pairs)
    vec_o[12:16, :] = jnp.zeros((4, width), f32)
    low_half, high_half = half_rows()
    half = lax.broadcasted_iota(jnp.int32, (QB, LANES), 1) < HEAD

    def attend(p, r):
        span = slice(r * length, (r + 1) * length)
        columns = columns_at(p)
        keys = now_v[1, span, :]
        values = now_v[2, span, :]
        keys_in = (keys * low_half + fk[r] * high_half, keys * high_half + fk[r] * low_half)
        one_low = jnp.broadcast_to(low_half, values.shape)
        one_high = jnp.broadcast_to(high_half, values.shape)
        values_in = (
            jnp.concatenate([values * low_half, one_low], axis=1),
            jnp.concatenate([values * high_half, one_high], axis=1),
        )

        def scores(j, h):
            part = slice(r * length + j * QB, r * length + (j + 1) * QB)
            query = now_v[0, part, :]
            marks = fq[r, j * QB : (j + 1) * QB, :]
            mine, other = (low_half, high_half) if h == 0 else (high_half, low_half)
            return nt(query * mine + marks * other, keys_in[h])

        blocks = [(j, h) for j in range(length // QB) for h in range(2)]
        following = scores(*blocks[0])
        kept = []
        for number, (j, h) in enumerate(blocks):
            current = following
            if number + 1 < len(blocks):
                following = scores(*blocks[number + 1])
            part = slice(r * length + j * QB, r * length + (j + 1) * QB)
            if r == rows - 1:
                share = rows * length // len(blocks)
                project(jnp.minimum(p + 1, pairs - 1), slice(number * share, (number + 1) * share))
            peak = jnp.max(current, axis=1, keepdims=True)
            soft = jnp.exp(current - peak).astype(bf16)
            kept.append((peak, nn(soft, values_in[h])))
            if h == 1:
                both = kept[0][1] + kept[1][1]
                total = both[:, LANES:]
                mix_v[part, columns] = (both[:, :LANES] / total).astype(bf16)
                logs = jnp.where(half, kept[0][0], kept[1][0]) + jnp.log(total)
                logs = pltpu.roll(logs, HEAD, 1)
                marks = fq[r, j * QB : (j + 1) * QB, :].astype(f32)
                feat_v[part, columns] = part_columns(-logs, marks).astype(bf16)
                kept = []

    schedule = (
        ((1, 4), (2, 2), (2, 3), (3, 1)),
        ((4, 1), (3, 2), (3, 3), (5, 1)),
        ((2, 4),),
        ((4, 2),),
        ((3, 4), (5, 2)),
        ((4, 3),),
        ((5, 3),),
        ((4, 4), (5, 4)),
    )
    def pair_out(p, which):
        columns = columns_at(p)
        found = [(now_v, qkv_o.at[p])] if which == 0 else [
            (mix_v.at[:, columns], mix_o.at[:, columns]),
            (feat_v.at[:, columns], feat_o.at[:, columns]),
        ]
        if comm and which == 1:
            found.append((ga.at[p], ga_o.at[p]))
        return [
            pltpu.make_async_copy(src, dst, loc.at[p, 3 * which + k])
            for k, (src, dst) in enumerate(found)
        ]

    def pair(p, carry):
        @pl.when(p > 0)
        def _():
            for copy in pair_out(p - 1, 0):
                copy.wait()

        now_v[...] = next_v[...]
        for copy in pair_out(p, 0):
            copy.start()
        for r in range(rows):
            attend(p, r)
            if comm:
                for number in range(pairs):
                    steps = schedule[rows * number + r]
                    pl.when(p == number)(functools.partial(transfer, *steps))
        for copy in pair_out(p, 1):
            copy.start()
        return carry

    lax.fori_loop(0, pairs, pair, 0)
    copies = pair_out(pairs - 1, 0)
    if comm:
        last = [
            pltpu.make_async_copy(src, dst, loc.at[pairs, 2 + k])
            for k, (src, dst) in enumerate(((gb, gb_o), (gc, gc_o)))
        ]
        for copy in last:
            copy.start()
        copies += last
        for group in gathers:
            group.finish()
    for p in range(pairs):
        copies += pair_out(p, 1)
    for copy in copies:
        copy.wait()


def row_mean(value):
    return jnp.mean(value, axis=-1, keepdims=True)


def column_sum(value):
    return jnp.sum(value, axis=0, keepdims=True)


def middle_kernel(
    seg, vec, x_hbm, mix_hbm, dual_hbm, cs_hbm, cd_hbm, gb_hbm, gc_hbm,
    so_o, do_o, one_o, gm_o, pg_o, vg_o,
    x_v, mix_v, dual_v, cs_v, cd_v, gb, gc, low_v, spread_v, two_v, ffn_v, hid_v, slope_v, pg_v,
    attn_v, sum_v,
    in_sem, out_sem, w_sem,
):
    rows, length = seg.shape
    tokens, width = x_v.shape
    blocks = hid_v.shape[0]
    step_rows = width // SLOTS
    tile = 512
    tiles = tokens // tile
    per_row = length // tile

    def rows_of(t, size=tile):
        return pl.ds(pl.multiple_of(t * size, size), size)

    w_copies = [
        pltpu.make_async_copy(gb_hbm, gb, w_sem.at[0]),
        pltpu.make_async_copy(gc_hbm, gc, w_sem.at[1]),
    ]
    pairs_in = ((mix_hbm, mix_v), (x_hbm, x_v), (cs_hbm, cs_v), (cd_hbm, cd_v), (dual_hbm, dual_v))

    def in_copy(k, t):
        src, dst = pairs_in[k]
        return pltpu.make_async_copy(src.at[rows_of(t)], dst.at[rows_of(t)], in_sem.at[k, t])

    w_copies[0].start()
    for k in range(5):
        in_copy(k, 0).start()
    w_copies[1].start()
    for t in range(1, tiles):
        for k in range(5):
            in_copy(k, t).start()
    pairs_out = ((cs_v, so_o), (dual_v, do_o), (dual_v, one_o), (ffn_v, gm_o))

    def out_copy(k, t):
        src, dst = pairs_out[k]
        return pltpu.make_async_copy(src.at[rows_of(t)], dst.at[rows_of(t)], out_sem.at[k, t])

    vg_o[...] = jnp.zeros_like(vg_o)
    gain_one, shift_one, gain_two, shift_two = (vec[k : k + 1, :] for k in range(4))
    bias_o, bias_d = vec[6:7, :], vec[7:8, :]
    w_copies[0].wait()
    w_copies[1].wait()
    lane = lax.broadcasted_iota(jnp.int32, (1, width), 1)

    def proj_weight():
        return merged(gb[:, :, :, 0:step_rows, :])

    def up_weight(f):
        return merged(gb[:, :, :, (f + 1) * step_rows : (f + 2) * step_rows, :])

    def down_weight(f):
        return merged(gc[f])

    def first_half(t):
        here = rows_of(t)
        attn = nn(mix_v[here, :], proj_weight()) + bias_o
        first_sum = x_v[here, :].astype(f32) + attn
        centred = first_sum - row_mean(first_sum)
        spread = lax.rsqrt(row_mean(centred * centred) + NORM_EPS)
        hat = centred * spread
        x_v[here, :] = hat.astype(bf16)
        spread_v[here, :] = jnp.broadcast_to(spread, (tile, LANES))
        first_norm = hat * gain_one + shift_one
        low_v[here, :] = first_norm.astype(bf16)
        two_v[here, :] = first_norm
        attn_v[...] = attn

    def feed(t):
        here = rows_of(t)
        first_low = low_v[here, :]
        ffn = bias_d
        upper = nn(first_low, up_weight(0))
        for f in range(blocks):
            u = upper + vec[8 + f : 9 + f, :]
            if f + 1 < blocks:
                upper = nn(first_low, up_weight(f + 1))
            square = u * u
            inner = jnp.tanh(u * (0.7978845608028654 + 0.035677408136300125 * square))
            share = 0.5 + 0.5 * inner
            hidden = u * share
            slope = share + hidden * (1.0 - share) * (
                1.5957691216057308 + 0.21406444881780073 * square
            )
            hidden = hidden.astype(bf16)
            hid_v[f, here, :] = hidden
            slope_v[f, here, :] = slope.astype(bf16)
            ffn = ffn + nn(hidden, down_weight(f))
        sum_v[...] = ffn

    def second_half(t):
        here = rows_of(t)
        attn = attn_v[...]
        ffn = sum_v[...]
        dual_v[here, :] = dual_v[here, :] + attn + ffn
        second_sum = two_v[here, :] + ffn
        centred = second_sum - row_mean(second_sum)
        spread = lax.rsqrt(row_mean(centred * centred) + NORM_EPS)
        hat = centred * spread
        second_norm = hat * gain_two + shift_two
        cot = cs_v[here, :].astype(f32)
        cs_v[here, :] = second_norm.astype(bf16)
        r = t // per_row
        ids = seg[pl.ds(r, 1), pl.ds(pl.multiple_of((t - r * per_row) * tile, tile), tile)]
        valid = jnp.where(ids != 0, 1.0, 0.0)
        valid = jnp.transpose(jnp.broadcast_to(valid, (LANES, tile)))[:, 0:1]
        counts = column_sum(valid) * width
        squares = [
            jnp.sum(column_sum(valid * (v * v)), axis=1, keepdims=True)
            for v in (second_norm, attn, ffn)
        ]
        line = jnp.where(lane == 0, counts, 0.0)
        for k in range(3):
            line = jnp.where(lane == k + 1, squares[k], line)
        vg_o[12:13, :] += line
        scaled = cot * gain_two
        grad = (scaled - row_mean(scaled) - hat * row_mean(scaled * hat)) * spread
        two_v[here, :] = grad
        vg_o[2:3, :] += column_sum(cot * hat)
        vg_o[3:4, :] += column_sum(cot)
        grad_low = (grad + cd_v[here, :].astype(f32)).astype(bf16)
        ffn_v[here, :] = grad_low
        vg_o[7:8, :] += column_sum(grad_low.astype(f32))

    def arrived(t, kinds):
        for k in kinds:
            in_copy(k, t).wait()

    def leave(t, kinds):
        for k in kinds:
            out_copy(k, t).start()

    def forward(t, carry):
        arrived(t, (0, 1, 2, 3, 4))
        first_half(t)
        feed(t)
        second_half(t)
        leave(t, (0, 1))
        return carry

    lax.fori_loop(0, tiles, forward, 0)

    pg_copies = []

    def pg_out(*where):
        copy = pltpu.make_async_copy(pg_v.at[where], pg_o.at[where], w_sem.at[len(pg_copies) + 2])
        copy.start()
        pg_copies.append(copy)

    every = slice(None)
    def back_hidden(f, carry):
        total = jnp.zeros((1, width), f32)
        for t in range(tokens // 512):
            here = slice(t * 512, (t + 1) * 512)
            grad = nt(ffn_v[here, :], down_weight(f))
            grad_up = (slope_v[f, here, :].astype(f32) * grad).astype(bf16)
            slope_v[f, here, :] = grad_up
            total = total + column_sum(grad_up.astype(f32))
        vg_o[pl.ds(8 + f, 1), :] = total
        return carry

    lax.fori_loop(0, blocks, back_hidden, 0)

    def weight_grads(f, carry):
        down = tn(hid_v[f], ffn_v[...])
        pg_v[f, :, :, 5 * step_rows :, :] = down.astype(bf16).reshape(4, 2, 4 * step_rows, width)
        up = tn(low_v[...], slope_v[f])
        rows_f = pl.ds(pl.multiple_of((f + 1) * step_rows, step_rows), step_rows)
        pg_v[:, :, :, rows_f, :] = up.astype(bf16).reshape(4, 4, 2, step_rows, width)
        return carry

    lax.fori_loop(0, blocks, weight_grads, 0)
    pg_out(every, every, every, slice(step_rows, 9 * step_rows))

    def grad_of_first(t):
        here = rows_of(t)
        grad = two_v[here, :]
        for f in range(blocks):
            grad = grad + nt(slope_v[f, here, :], up_weight(f))
        sum_v[...] = grad

    def back_first(t):
        here = rows_of(t)
        grad = sum_v[...]
        hat = x_v[here, :].astype(f32)
        scaled = grad * gain_one
        spread = spread_v[here, 0:1]
        grad_one = (scaled - row_mean(scaled) - hat * row_mean(scaled * hat)) * spread
        dual_v[here, :] = grad_one
        grad_low = (grad_one + cd_v[here, :].astype(f32)).astype(bf16)
        low_v[here, :] = grad_low
        ffn_v[here, :] = nt(grad_low, proj_weight()).astype(bf16)
        vg_o[0:1, :] += column_sum(grad * hat)
        vg_o[1:2, :] += column_sum(grad)
        vg_o[6:7, :] += column_sum(grad_low.astype(f32))

    for t in range(tiles):
        out_copy(1, t).wait()

    def backward(t, carry):
        grad_of_first(t)
        back_first(t)
        leave(t, (2, 3))
        return carry

    lax.fori_loop(0, tiles, backward, 0)
    proj = tn(mix_v[...], low_v[...])
    pg_v[:, :, :, 0:step_rows, :] = proj.astype(bf16).reshape(4, 4, 2, step_rows, width)
    pg_out(every, every, every, slice(0, step_rows))
    for t in range(tiles):
        for k in (0, 2, 3):
            out_copy(k, t).wait()
    for copy in pg_copies:
        copy.wait()


class Scatter:
    def __init__(self, here, send, mine, bufs, send_sem, recv_sem, straight):
        self.here, self.source, self.mine = here, send, mine
        self.from_core, self.from_b, self.from_a, self.from_z = bufs
        self.send_sem, self.recv_sem, self.straight = send_sem, recv_sem, straight
        self.last = 2 if straight else 3

    def copies(self, phase):
        me, mine = self.here, self.mine
        if phase == 0:
            base, found = 0, [(self.source, self.from_core, me.to_core)]
        elif phase == self.last:
            base = 4
            found = [
                (mine.at[me.dp, me.zs[k]], self.from_z.at[k - 1], me.to_z[k]) for k in range(1, 4)
            ]
        elif self.straight:
            base = 1
            found = [
                (mine.at[me.ab], self.from_a, me.to_ab),
                (mine.at[me.a], self.from_b.at[0], me.to_a),
                (mine.at[me.b], self.from_b.at[1], me.to_b),
            ]
        elif phase == 1:
            base = 1
            found = [
                (mine.at[me.b], self.from_b.at[0], me.to_b),
                (mine.at[me.ab], self.from_b.at[1], me.to_b),
            ]
        else:
            base, found = 3, [(mine.at[me.a], self.from_a, me.to_a)]
        return [
            remote(src, dst, self.send_sem.at[base + k], self.recv_sem.at[base + k], device)
            for k, (src, dst, device) in enumerate(found)
        ]

    def start(self, phase):
        for copy in self.copies(phase):
            copy.start()

    def add(self, phase):
        me, mine = self.here, self.mine
        for copy in self.copies(phase):
            copy.wait_recv()

        def into(where, *parts):
            if len(parts) == 1:
                mine[where] = mine[where] + parts[0]
            else:
                total = mine[where].astype(f32)
                for part in parts:
                    total = total + part.astype(f32)
                mine[where] = total.astype(bf16)

        for z in range(4):
            if phase == 0:
                for d in range(4):
                    into((d, z), self.from_core[d, z])
            elif self.straight:
                into((me.dp, z), self.from_a[z], self.from_b[0, z], self.from_b[1, z])
            elif phase == 1:
                into((me.dp, z), self.from_b[0, z])
                into((me.a, z), self.from_b[1, z])
            else:
                into((me.dp, z), self.from_a[z])

    def result(self):
        for copy in self.copies(self.last):
            copy.wait_recv()
        total = self.mine[self.here.dp, self.here.z].astype(f32)
        for k in range(3):
            total = total + self.from_z[k].astype(f32)
        return total

    def finish(self):
        for phase in range(self.last + 1):
            for copy in self.copies(phase):
                copy.wait_send()


class Total:
    def __init__(self, here, own, bufs, send_sem, recv_sem):
        self.here, self.own, self.bufs = here, own, bufs
        self.send_sem, self.recv_sem = send_sem, recv_sem

    def copies(self, phase):
        me, bufs = self.here, self.bufs
        if phase == 0:
            found = [(self.own, bufs.at[0], 0, me.to_core)]
        else:
            slot = 1 + me.dp if phase == 1 else 5 + me.z
            devices = [me.to_a, me.to_b, me.to_ab] if phase == 1 else me.to_z[1:]
            found = [(bufs.at[slot], bufs.at[slot], slot, device) for device in devices]
        return [
            remote(src, dst, self.send_sem.at[3 * phase + k], self.recv_sem.at[slot], device)
            for k, (src, dst, slot, device) in enumerate(found)
        ]

    def start(self, phase):
        for copy in self.copies(phase):
            copy.start()

    def arrive(self, *slots):
        for slot in slots:
            ref = self.bufs.at[slot]
            remote(ref, ref, self.send_sem.at[0], self.recv_sem.at[slot], self.here.to_core).wait_recv()

    def add(self, phase):
        me, bufs = self.here, self.bufs
        if phase == 0:
            self.arrive(0)
            bufs[1 + me.dp] = self.own[...] + bufs[0]
        else:
            self.arrive(1 + me.a, 1 + me.b, 1 + me.ab)
            bufs[5 + me.z] = bufs[1] + bufs[2] + bufs[3] + bufs[4]

    def result(self):
        self.arrive(*[5 + self.here.zs[k] for k in range(1, 4)])
        bufs = self.bufs
        return bufs[5] + bufs[6] + bufs[7] + bufs[8]

    def finish(self):
        for phase in range(3):
            for copy in self.copies(phase):
                copy.wait_send()


def backward_kernel(comm, scale, *refs):
    (seg, vg, qkv_hbm, feat_hbm, mix_hbm, gm_hbm, one_hbm, x_hbm, ga_hbm) = refs[:9]
    if comm:
        (pg_hbm, sg_o, tot_o, totq_o, vg_o) = refs[9:14]
        refs = refs[14:]
    else:
        (sg_o, pq_o, vg_o) = refs[9:12]
        refs = refs[12:]
    (qkv_v, feat_v, mix_v, gm_v, one_v, x_v, ga, gq_v, fk, pq_v, in_sem, w_sem, out_sem) = refs[:13]
    rows, length = seg.shape
    tokens, width = x_v.shape
    pairs = width // LANES
    step_rows = width // SLOTS

    def pair_copies(p):
        columns = pl.ds(pl.multiple_of(p * LANES, LANES), LANES)
        found = [(qkv_hbm.at[p], qkv_v.at[p])]
        found += [
            (src.at[:, columns], dst.at[:, columns])
            for src, dst in ((gm_hbm, gm_v), (mix_hbm, mix_v), (feat_hbm, feat_v))
        ]
        return [
            pltpu.make_async_copy(src, dst, in_sem.at[p, k]) for k, (src, dst) in enumerate(found)
        ]

    late = [
        pltpu.make_async_copy(src, dst, w_sem.at[k])
        for k, (src, dst) in enumerate(((x_hbm, x_v), (ga_hbm, ga), (one_hbm, one_v)))
    ]
    if comm:
        (mine, fc, fb, fa, fz, mine_q, qc, qb, qa, qz, vp, vb, s1, r1, s2, r2, s3, r3) = refs[13:]
        here = Place()
        here.greet()
        weights = [
            Scatter(
                here,
                pg_hbm.at[:, :, 1 - here.c, pl.ds(g * 3 * step_rows, 3 * step_rows)],
                mine.at[g],
                (fc.at[g], fb.at[g], fa.at[g], fz.at[g]),
                s1.at[g],
                r1.at[g],
                False,
            )
            for g in range(3)
        ]
        columns_of = [
            Scatter(
                here,
                pq_v.at[p, :, :, 1 - here.c],
                mine_q.at[p],
                (qc.at[p], qb.at[p], qa.at[p], qz.at[p]),
                s2.at[p],
                r2.at[p],
                True,
            )
            for p in range(pairs)
        ]
        sums = Total(here, vp, vb, s3, r3)
        vp[...] = vg[...]
        mine_copies = [
            pltpu.make_async_copy(
                pg_hbm.at[:, :, here.c, pl.ds(g * 3 * step_rows, 3 * step_rows)], mine.at[g], w_sem.at[3 + g]
            )
            for g in range(3)
        ]
    if not comm:
        vg_o[...] = vg[...]
    vector = vp if comm else vg_o
    for copy in pair_copies(0):
        copy.start()
    if comm:
        for copy in mine_copies:
            copy.start()
    for p in range(1, pairs):
        for copy in pair_copies(p):
            copy.start()
    for copy in late:
        copy.start()
    for r in range(rows):
        fk[r] = segment_columns(seg[r : r + 1, :])[1]
    if comm:
        here.greeted()
        for group in weights:
            group.start(0)
    low_half, high_half = half_rows()

    def transfer(number):
        if number == 0:
            for copy in mine_copies:
                copy.wait()
        for group, steps in list(zip(weights, ((0, 2, 3), (1, 3, 4), (3, 5, 6)))) + [
            (columns_of[p], (rows * p + rows, rows * p + rows + 1)) for p in range(pairs)
        ]:
            for phase in range(group.last):
                if number == steps[phase]:
                    group.add(phase)
                    group.start(phase + 1)
        for p in range(pairs):
            if number == rows * (p + 1) - 1:
                columns_of[p].start(0)
                mine_q[p] = pq_v[p, :, :, here.c]
        if number == rows * pairs - 1:
            sums.start(0)

    def attend(i, carry):
        p = i // rows
        r = lax.rem(i, rows)
        span = pl.ds(pl.multiple_of(r * length, length), length)
        columns = pl.ds(pl.multiple_of(p * LANES, LANES), LANES)

        @pl.when(r == 0)
        def _():
            for copy in pair_copies(p):
                copy.wait()

        queries = qkv_v[p, 0, span, :]
        keys = qkv_v[p, 1, span, :]
        values = qkv_v[p, 2, span, :]
        grads = gm_v[span, columns]
        marks = feat_v[span, columns]
        product = grads.astype(f32) * mix_v[span, columns].astype(f32)
        is_low = lax.broadcasted_iota(jnp.int32, product.shape, 1) < HEAD
        for_low = jnp.sum(jnp.where(is_low, product, 0.0), axis=1, keepdims=True)
        for_high = jnp.sum(jnp.where(is_low, 0.0, product), axis=1, keepdims=True)
        deltas = part_columns(-jnp.where(is_low, for_high, for_low), 0.0).astype(bf16)
        place = lax.rem(lax.broadcasted_iota(jnp.int32, (1, LANES), 1), HEAD)
        ones = jnp.where((place >= 16) & (place < 19), 1.0, 0.0).astype(bf16)
        queries_t = jnp.transpose(queries)
        grads_t = jnp.transpose(grads)
        key_parts, value_parts = [], []
        query_grads = [None] * (length // QB)
        for h in range(2):
            mine_h, other_h = (low_half, high_half) if h == 0 else (high_half, low_half)
            half = slice(h * HEAD, (h + 1) * HEAD)
            key_own = keys * mine_h
            key_in = key_own + fk[r] * other_h
            value_in = values * mine_h + ones * other_h
            key_sum = value_sum = None
            for j in range(length // QB):
                part = slice(j * QB, (j + 1) * QB)
                soft = jnp.exp(nt(queries[part] * mine_h + marks[part] * other_h, key_in))
                wide = nt(grads[part] * mine_h + deltas[part] * other_h, value_in)
                back = (soft * wide).astype(bf16)
                soft = soft.astype(bf16)
                moved = nn(back, key_own)
                query_grads[j] = moved if h == 0 else query_grads[j] + moved
                value_part = nn(grads_t[half, part], soft)
                key_part = nn(queries_t[half, part], back)
                value_sum = value_part if j == 0 else value_sum + value_part
                key_sum = key_part if j == 0 else key_sum + key_part
            key_parts.append(key_sum)
            value_parts.append(value_sum)
        for j in range(length // QB):
            part = pl.ds(pl.multiple_of(r * length + j * QB, QB), QB)
            gq_v[0, part, columns] = (query_grads[j] * scale).astype(bf16)
        gq_v[1, span, columns] = jnp.transpose(jnp.concatenate(key_parts, axis=0)).astype(bf16)
        gq_v[2, span, columns] = jnp.transpose(jnp.concatenate(value_parts, axis=0)).astype(bf16)

        @pl.when(r == rows - 1)
        def _():
            @pl.when(p == 0)
            def _():
                late[0].wait()

            stacked = jnp.concatenate([gq_v[j, :, columns] for j in range(3)], axis=1)
            for k, j in ((4, 0), (5, 2)):
                part = stacked[:, j * LANES : (j + 1) * LANES].astype(f32)
                vector[k : k + 1, columns] = column_sum(part)
            grad = tn(x_v[...], stacked).astype(bf16).reshape(4, 4, 2, step_rows, 3 * LANES)
            for j in range(3):
                pq_v[p, :, :, :, j * step_rows : (j + 1) * step_rows, :] = grad[
                    ..., j * LANES : (j + 1) * LANES
                ]

        if comm:
            for number in range(rows * pairs):
                pl.when(i == number)(functools.partial(transfer, number))
        return carry

    lax.fori_loop(0, rows * pairs, attend, 0)
    late[1].wait()
    late[2].wait()

    if not comm:
        pq_copy = pltpu.make_async_copy(pq_v, pq_o, out_sem.at[4])
        pq_copy.start()

    def out_copy(t):
        span = pl.ds(pl.multiple_of(t * 512, 512), 512)
        return pltpu.make_async_copy(one_v.at[span, :], sg_o.at[span, :], out_sem.at[t])

    def stream(t):
        span = pl.ds(t * 512, 512)
        total = one_v[span, :]
        for j in range(3):
            total = total + nt(
                gq_v[j, span, :],
                jnp.concatenate(
                    [merged(ga[p, :, :, :, :, j * LANES : (j + 1) * LANES]) for p in range(pairs)],
                    axis=1,
                ),
            )
        one_v[span, :] = total
        out_copy(t).start()

    for t in range(tokens // 512):
        stream(t)
        if comm:
            transfer(rows * pairs + t)
            if t < 2:
                sums.add(t)
                sums.start(t + 1)
    if comm:
        for g in range(3):
            tot_o[g * 3 * step_rows : (g + 1) * 3 * step_rows, :] = weights[g].result()
        for p in range(pairs):
            totq_o[p] = columns_of[p].result()
        vg_o[...] = sums.result()
        for group in columns_of + weights + [sums]:
            group.finish()
    else:
        pq_copy.wait()
    for t in range(tokens // 512):
        out_copy(t).wait()


def adam(weight, gradient, first_old, second, rates):
    step_rate, decay_rate = rates
    first_new = BETA_FIRST * first_old + (1.0 - BETA_FIRST) * gradient
    second_new = BETA_SECOND * second + (1.0 - BETA_SECOND) * gradient * gradient
    first_hat = first_new / (1.0 - BETA_FIRST**STEP)
    second_hat = second_new / (1.0 - BETA_SECOND**STEP)
    updated = weight - step_rate * (
        first_hat / (jnp.sqrt(second_hat) + ADAM_EPS) + decay_rate * weight
    )
    return second_new, updated


def update_kernel(tot, totq, vg, sg_hbm, *refs):
    weights, firsts, seconds = refs[0:5], refs[5:10], refs[10:15]
    sg_o, root, grads, renewed, updated = refs[15], refs[16], refs[17:22], refs[22:27], refs[27:32]
    sg_v, sem = refs[32:]
    size = sg_hbm.shape[0] // 8
    copies = []
    for t in range(8):
        span = pl.ds(t * size, size)
        copies.append(pltpu.make_async_copy(sg_hbm.at[span], sg_v.at[span], sem.at[0, t]))
        copies.append(pltpu.make_async_copy(sg_v.at[span], sg_o.at[span], sem.at[1, t]))
    for copy in copies[0::2]:
        copy.start()
    width = tot.shape[1]
    step_rows = width // SLOTS
    pairs = width // LANES

    def apply(k, columns, gradient):
        where = (slice(None), columns)
        grads[k][where] = gradient
        renewed[k][where], updated[k][where] = adam(
            weights[k][where], gradient, firsts[k][where], seconds[k][where], RATES[k]
        )

    for j in range(3):
        for p in range(pairs):
            begin = j * width + p * LANES
            apply(0, slice(begin, begin + LANES), totq[p, j * step_rows : (j + 1) * step_rows, :])
    apply(1, slice(None), tot[0:step_rows, :])
    for j in range(4):
        apply(2, slice(j * width, (j + 1) * width), tot[(j + 1) * step_rows : (j + 2) * step_rows, :])
    apply(3, slice(None), tot[5 * step_rows :, :])
    for t in range(8):
        copies[2 * t].wait()
        copies[2 * t + 1].start()
    count = weights[4].shape[1]
    begin = (lax.axis_index("dp") * 8 + lax.axis_index("fsdp")) * count
    top = begin // width
    shift = begin - top * width
    row = lax.broadcasted_iota(jnp.int32, vg.shape, 0)
    lane = lax.broadcasted_iota(jnp.int32, vg.shape, 1)
    kept = ((row == top) & (lane >= shift)) | ((row == top + 1) & (lane < shift))
    line = column_sum(jnp.where(kept, vg[...], 0.0))
    line = pltpu.roll(jnp.broadcast_to(line, (8, width)), lax.rem(width - shift, width), 1)
    apply(4, slice(None), line[0:1, :count])
    sums = vg[12:13, 0:LANES]
    means = jnp.sqrt(sums / sums[:, 0:1])
    lane = lax.broadcasted_iota(jnp.int32, means.shape, 1)
    for k in range(3):
        root[k] = jnp.sum(jnp.where(lane == k + 1, means, 0.0))
    for copy in copies[1::2]:
        copy.wait()


def params(**more):
    return pltpu.CompilerParams(vmem_limit_bytes=62 * 2**20, **more)


def shape(dims, kind):
    return jax.ShapeDtypeStruct(dims, kind)


def pack_columns(full, blocks):
    width = full.shape[0]
    parts = full.reshape(SLOTS, width // SLOTS, blocks, width)
    return jnp.swapaxes(parts, 1, 2).reshape(SLOTS, -1, width)


def unpack_columns(packed, blocks):
    width = packed.shape[-1]
    parts = packed.reshape(SLOTS, blocks, width // SLOTS, width)
    return jnp.swapaxes(parts, 1, 2).reshape(width, blocks * width)


def per_device(comm, *args):
    (stream_in, dual_in, segment_ids) = args[:3]
    weights, firsts, seconds = args[3:8], args[8:13], args[13:18]
    cot_stream, cot_dual = args[18:]
    tokens, width = stream_in.shape
    rows, length = segment_ids.shape
    pairs = width // LANES
    hidden = weights[2].shape[1]
    blocks = hidden // width
    unit = width // SLOTS
    scale = HEAD**-0.5
    slots = (4, 4, 2)
    dma = pltpu.SemaphoreType.DMA
    sem_gather = [dma((10,)), dma((12,))]
    ga_shape = (pairs,) + slots + (unit, 4 * LANES)
    gb_shape, gc_shape = (slots + (n, width) for n in (5 * unit, 4 * unit))

    def vm(dims, kind=bf16):
        return pltpu.VMEM(dims, kind)

    flat = (tokens, width)
    common_out = [
        shape((pairs, 3, tokens, LANES), bf16),
        shape(flat, bf16),
        shape(flat, bf16),
        shape((16, width), f32),
    ]
    common_scratch = [
        vm(flat),
        vm((3, tokens, LANES)),
        vm((3, tokens, LANES)),
        vm(flat),
        vm(flat),
        vm((rows, length, LANES)),
        vm((rows, length, LANES)),
        vm(ga_shape),
    ]
    cost = pl.CostEstimate(flops=8 * 10**9, bytes_accessed=2 * 10**7, transcendentals=2 * 10**7)
    if comm:
        masters = [w if w.ndim == 2 else w.reshape(1, -1) for w in weights]
        qkv, mix, feat, vec, ga, gb, gc = pl.pallas_call(
            functools.partial(forward_kernel, True, scale),
            out_shape=common_out + [shape(s, bf16) for s in (ga_shape, gb_shape, gc_shape)],
            in_specs=[ANY] + [VMEM] * 6,
            out_specs=[ANY] * 3 + [VMEM] + [ANY] * 3,
            scratch_shapes=common_scratch
            + [vm(gb_shape), vm(gc_shape), dma((pairs + 1, 6))]
            + [dma((pairs, 10)), dma((pairs, 12))]
            + sem_gather * 2,
            compiler_params=params(collective_id=0, has_side_effects=True),
            cost_estimate=cost,
            name="gather_forward",
        )(stream_in, segment_ids, *masters)
    else:
        full = [lax.all_gather(w.astype(bf16), AXES, axis=0, tiled=True) for w in weights]
        packed = pack_columns(full[0], 3).reshape(SLOTS, 3, unit, pairs, LANES)
        packed = packed.transpose(3, 0, 2, 1, 4).reshape(pairs, SLOTS, unit, 3 * LANES)
        vec_pad = jnp.pad(full[4].reshape(SLOTS, -1), ((0, 0), (0, HEAD))).reshape(SLOTS, 2, LANES)
        vec_pad = jnp.pad(vec_pad[None], ((0, pairs - 1), (0, 0), (0, unit - 2), (0, 0)))
        ga = jnp.concatenate([packed, vec_pad], axis=3).reshape(ga_shape)
        gb = jnp.concatenate(
            [pack_columns(full[1], 1), pack_columns(full[2], blocks)], axis=1
        ).reshape(gb_shape)
        gc = full[3].reshape(gc_shape)
        qkv, mix, feat, vec = pl.pallas_call(
            functools.partial(forward_kernel, False, scale),
            out_shape=common_out,
            in_specs=[ANY, VMEM, ANY],
            out_specs=[ANY] * 3 + [VMEM],
            scratch_shapes=common_scratch + [dma((pairs + 1, 6))],
            compiler_params=params(),
            cost_estimate=cost,
            name="forward",
        )(stream_in, segment_ids, ga)

    pg_shape = slots + (9 * unit, width)
    tiles = tokens // 512
    stream_out, dual_out, grad_one, grad_mixed, pg, vg = pl.pallas_call(
        middle_kernel,
        out_shape=[
            shape(flat, bf16),
            shape(flat, f32),
            shape(flat, f32),
            shape(flat, bf16),
            shape(pg_shape, bf16),
            shape((16, width), f32),
        ],
        in_specs=[VMEM, VMEM] + [ANY] * 7,
        out_specs=[ANY] * 5 + [VMEM],
        scratch_shapes=[
            vm(flat),
            vm(flat),
            vm(flat, f32),
            vm(flat),
            vm(flat),
            vm(gb_shape),
            vm(gc_shape),
            vm(flat),
            vm((tokens, LANES), f32),
            vm(flat, f32),
            vm(flat),
            vm((blocks, tokens, width)),
            vm((blocks, tokens, width)),
            vm(pg_shape),
            vm((512, width), f32),
            vm((512, width), f32),
            dma((5, tiles)),
            dma((4, tiles)),
            dma((12,)),
        ],
        compiler_params=params(),
        cost_estimate=pl.CostEstimate(
            flops=3 * 10**10, bytes_accessed=4 * 10**7, transcendentals=4 * 10**6
        ),
        name="feed_forward",
    )(segment_ids, vec, stream_in, mix, dual_in, cot_stream, cot_dual, gb, gc)

    pq_shape = (pairs,) + slots + (3 * unit, LANES)
    scratch = [
        vm((pairs, 3, tokens, LANES)),
        vm(flat),
        vm(flat),
        vm(flat),
        vm(flat, f32),
        vm(flat),
        vm(ga_shape),
        vm((3,) + flat),
        vm((rows, length, LANES)),
        vm(pq_shape),
        dma((pairs, 4)),
        dma((6,)),
        dma((8,)),
    ]
    operands = (segment_ids, vg, qkv, feat, mix, grad_mixed, grad_one, stream_in, ga)
    cost = pl.CostEstimate(flops=2 * 10**10, bytes_accessed=3 * 10**7, transcendentals=2 * 10**7)
    if comm:
        tail = (9 * unit, width)
        tail_q = (3 * unit, LANES)
        stream_grad, tot, totq, vg = pl.pallas_call(
            functools.partial(backward_kernel, True, scale),
            out_shape=[
                shape(flat, f32),
                shape(tail, f32),
                shape((pairs,) + tail_q, f32),
                shape((16, width), f32),
            ],
            in_specs=[VMEM, VMEM] + [ANY] * 8,
            out_specs=[ANY] + [VMEM] * 3,
            scratch_shapes=scratch
            + [vm((3,) + s + (3 * unit, width)) for s in ((4, 4), (4, 4), (2, 4), (4,), (3,))]
            + [vm((pairs,) + s + tail_q) for s in ((4, 4), (4, 4), (2, 4), (4,), (3,))]
            + [vm((16, width), f32), vm((9, 16, width), f32)]
            + [dma((3, 7)), dma((3, 7)), dma((pairs, 7)), dma((pairs, 7)), dma((9,)), dma((9,))],
            compiler_params=params(collective_id=1, has_side_effects=True),
            cost_estimate=cost,
            name="backward_scatter",
        )(*operands, pg)
        outs = pl.pallas_call(
            update_kernel,
            out_shape=[shape(flat, f32), shape((3,), f32)]
            + [shape(w.shape, f32) for _ in range(3) for w in masters],
            in_specs=[VMEM] * 3 + [ANY] + [VMEM] * 15,
            out_specs=[ANY, pl.BlockSpec(memory_space=pltpu.SMEM)] + [VMEM] * 15,
            scratch_shapes=[vm(flat, f32), dma((2, 8))],
            compiler_params=params(),
            name="update",
        )(tot, totq, vg, stream_grad, *masters, *firsts[:4], firsts[4].reshape(1, -1), *seconds[:4], seconds[4].reshape(1, -1))
        stream_grad, root_means = outs[:2]
        grads, renewed, updated = (
            [v.reshape(w.shape) for v, w in zip(outs[k : k + 5], weights)] for k in (2, 7, 12)
        )
    else:
        stream_grad, pq, vg = pl.pallas_call(
            functools.partial(backward_kernel, False, scale),
            out_shape=[shape(flat, f32), shape(pq_shape, bf16), shape((16, width), f32)],
            in_specs=[VMEM, VMEM] + [ANY] * 7,
            out_specs=[ANY, ANY, VMEM],
            scratch_shapes=scratch,
            compiler_params=params(),
            cost_estimate=cost,
            name="backward",
        )(*operands)
        pq = jnp.moveaxis(pq.reshape(pairs, SLOTS, 3 * unit, LANES), 0, 2).reshape(SLOTS, 3 * unit, width)
        pg = pg.reshape(SLOTS, 9 * unit, width)
        partial = [
            unpack_columns(pq, 3),
            unpack_columns(pg[:, :unit], 1),
            unpack_columns(pg[:, unit : 5 * unit], blocks),
            pg[:, 5 * unit :].reshape(hidden, width),
            vg[:12].reshape(-1),
        ]
        grads = [
            lax.psum_scatter(g.astype(f32), AXES, scatter_dimension=0, tiled=True) for g in partial
        ]
        totals = lax.psum(vg[12, :4], AXES)
        root_means = jnp.sqrt(totals[1:] / totals[0])
        made = [adam(*four) for four in zip(weights, grads, firsts, seconds, RATES)]
        renewed, updated = ([m[k] for m in made] for k in range(2))
    return (stream_out, dual_out, stream_grad, root_means, *grads, *renewed, *updated)


def solution(mesh):
    sizes = dict(mesh.shape)
    comm = sizes["dp"] == 4 and sizes["fsdp"] == 8
    matrix, line = P(AXES, None), P(AXES)
    five = (matrix, matrix, matrix, matrix, line)
    in_specs = (matrix,) * 3 + five * 3 + (matrix, matrix)
    out_specs = (matrix,) * 3 + (P(),) + five * 3
    return jax.shard_map(
        functools.partial(per_device, comm),
        mesh=mesh,
        in_specs=in_specs,
        out_specs=out_specs,
        check_vma=False,
    )
```

profile of v0, /device:TPU:0, one launch (start us, length us, event | category | flops | bytes accessed | tf_op | source)
XLA Modules:
  0.0 186.5 jit_solution(10600432952752960815)
XLA Ops:
  0.7 57.0 %gather_forward.1 = (bf16[4,3,2048,128]{3,2,1,0:T(8,128)(2,1)}, bf16[2048,512]{1,0:T(8,128)(2,1)}, bf16[2048,512]{1,0:T(8,128)(2,1)}, f32[16,512]{1,0:T(8,128)},...) custom-call(bf16[2048,512]{1,0:T(8,128)(2,1)} %refs_7_.2, ...), custom_call_target="tpu_custom_call" | custom-call | flops 8000000000 | bytes 20000000 | tf_op jit(solution)/shard_map/gather_forward/pallas_call | solution.py:1098
  57.6 55.4 %feed_forward.1 = (bf16[2048,512]{1,0:T(8,128)(2,1)}, f32[2048,512]{1,0:T(8,128)}, f32[2048,512]{1,0:T(8,128)}, bf16[2048,512]{1,0:T(8,128)(2,1)}, bf16[4,4,2,14...) custom-call(s32[2,1024]{1,0:T(2,128)} %refs_0_.4, f32[16,512]{1,0:T(8,128)} %get-tuple-element.53.vec, ...), custom_call_target="tpu_custom_call" | custom-call | flops 30000001024 | bytes 40000000 | tf_op jit(solution)/shard_map/feed_forward/pallas_call | solution.py:1135
  113.0 67.1 %backward_scatter.1 = (f32[2048,512]{1,0:T(8,128)}, f32[144,512]{1,0:T(8,128)}, f32[4,48,128]{2,1,0:T(8,128)}, f32[16,512]{1,0:T(8,128)}) custom-call(s32[2,1024]{1,0:T(2,128)} %refs_0_.4, f32[16,512]{1,0:T(8,128)} %get-tuple-element.59.refs_1_, bf16[4,3,2048,128]{3,2,1,0:T(8,128)(2,1)} %get-tuple-element.60.refs_2_, ...), custom_call_target="tpu_custom_call" | custom-call | flops 20000000000 | bytes 30000000 | tf_op jit(solution)/shard_map/backward_scatter/pallas_call | solution.py:1196
  180.1 6.2 %update.1 = (f32[2048,512]{1,0:T(8,128)}, f32[3]{0:T(128)}, f32[16,1536]{1,0:T(8,128)}, f32[16,512]{1,0:T(8,128)}, f32[16,2048]{1,0:T(8,128)}, /*index=5*/f32[64...) custom-call(f32[144,512]{1,0:T(8,128)} %get-tuple-element.66.tot, ...), custom_call_target="tpu_custom_call" | custom-call | tf_op jit(solution)/shard_map/update/pallas_call | solution.py:1215
where the time goes:
time: 187 us; the launch traced here: 186 us
  Pallas kernels  186 us (99%)
    pallas_call x1, Pallas kernels, per_device(): pl.pallas_call(functools.partial(backward_kernel, True, scale), out_shape...  67.1 us
    pallas_call x1, Pallas kernels, per_device(): pl.pallas_call(functools.partial(forward_kernel, True, scale), out_shape=...  57 us
    pallas_call x1, Pallas kernels, per_device(): pl.pallas_call(middle_kernel, out_shape=[shape(flat, bf16), shape(flat, f...  55.4 us
    pallas_call x1, Pallas kernels, per_device(): pl.pallas_call(update_kernel, out_shape=[shape(flat, f32), shape((3,), f3...  6.18 us

commit v1 on v0

--- a/solution.py
+++ b/solution.py
@@ -237,9 +237,9 @@
             gathers[group].step(number)
 
     if comm:
-        transfer((0, 1), (4, 0), (1, 1))
+        transfer((0, 1), (1, 1))
         marks_of(0)
-        transfer((0, 2), (0, 3), (2, 1), (5, 0))
+        transfer((0, 2), (0, 3), (4, 0), (2, 1), (5, 0))
         for r in range(1, rows):
             marks_of(r)
         transfer((0, 4))
@@ -332,14 +332,15 @@
 
     schedule = (
         ((1, 4), (2, 2), (2, 3), (3, 1)),
-        ((4, 1), (3, 2), (3, 3), (5, 1)),
-        ((2, 4),),
+        ((4, 1), (3, 2), (3, 3)),
+        ((2, 4), (5, 1)),
         ((4, 2),),
-        ((3, 4), (5, 2)),
+        ((3, 4),),
+        ((5, 2),),
         ((4, 3),),
-        ((5, 3),),
-        ((4, 4), (5, 4)),
+        ((5, 3), (4, 4), (5, 4)),
     )
+
     def pair_out(p, which):
         columns = columns_at(p)
         found = [(now_v, qkv_o.at[p])] if which == 0 else [
@@ -426,10 +427,12 @@
         src, dst = pairs_in[k]
         return pltpu.make_async_copy(src.at[rows_of(t)], dst.at[rows_of(t)], in_sem.at[k, t])
 
+    in_copy(0, 0).start()
+    in_copy(1, 0).start()
     w_copies[0].start()
-    for k in range(5):
+    w_copies[1].start()
+    for k in range(2, 5):
         in_copy(k, 0).start()
-    w_copies[1].start()
     for t in range(1, tiles):
         for k in range(5):
             in_copy(k, t).start()
@@ -443,7 +446,6 @@
     gain_one, shift_one, gain_two, shift_two = (vec[k : k + 1, :] for k in range(4))
     bias_o, bias_d = vec[6:7, :], vec[7:8, :]
     w_copies[0].wait()
-    w_copies[1].wait()
     lane = lax.broadcasted_iota(jnp.int32, (1, width), 1)
 
     def proj_weight():
@@ -534,8 +536,14 @@
             out_copy(k, t).start()
 
     def forward(t, carry):
-        arrived(t, (0, 1, 2, 3, 4))
+        arrived(t, (0, 1))
         first_half(t)
+
+        @pl.when(t == 0)
+        def _():
+            w_copies[1].wait()
+
+        arrived(t, (2, 3, 4))
         feed(t)
         second_half(t)
         leave(t, (0, 1))

time: 187 us -> 187 us (level)
  no operation moved by 1% of the time
where the time goes in v1:
time: 187 us; the launch traced here: 186 us
  Pallas kernels  186 us (99%)
    pallas_call x1, Pallas kernels, per_device(): pl.pallas_call(functools.partial(backward_kernel, True, scale), out_shape...  67.1 us
    pallas_call x1, Pallas kernels, per_device(): pl.pallas_call(functools.partial(forward_kernel, True, scale), out_shape=...  57.6 us
    pallas_call x1, Pallas kernels, per_device(): pl.pallas_call(middle_kernel, out_shape=[shape(flat, bf16), shape(flat, f...  54.6 us
    pallas_call x1, Pallas kernels, per_device(): pl.pallas_call(update_kernel, out_shape=[shape(flat, f32), shape((3,), f3...  6.18 us

profile of v1, /device:TPU:0, one launch (start us, length us, event | category | flops | bytes accessed | tf_op | source)
XLA Modules:
  0.0 186.4 jit_solution(17503164571102402039)
XLA Ops:
  0.7 57.6 %gather_forward.1 = (bf16[4,3,2048,128]{3,2,1,0:T(8,128)(2,1)}, bf16[2048,512]{1,0:T(8,128)(2,1)}, bf16[2048,512]{1,0:T(8,128)(2,1)}, f32[16,512]{1,0:T(8,128)},...) custom-call(bf16[2048,512]{1,0:T(8,128)(2,1)} %refs_7_.2, ...), custom_call_target="tpu_custom_call" | custom-call | flops 8000000000 | bytes 20000000 | tf_op jit(solution)/shard_map/gather_forward/pallas_call | solution.py:1106
  58.3 54.6 %feed_forward.1 = (bf16[2048,512]{1,0:T(8,128)(2,1)}, f32[2048,512]{1,0:T(8,128)}, f32[2048,512]{1,0:T(8,128)}, bf16[2048,512]{1,0:T(8,128)(2,1)}, bf16[4,4,2,14...) custom-call(s32[2,1024]{1,0:T(2,128)} %refs_0_.4, f32[16,512]{1,0:T(8,128)} %get-tuple-element.53.vec, ...), custom_call_target="tpu_custom_call" | custom-call | flops 30000001024 | bytes 40000000 | tf_op jit(solution)/shard_map/feed_forward/pallas_call | solution.py:1143
  112.9 67.1 %backward_scatter.1 = (f32[2048,512]{1,0:T(8,128)}, f32[144,512]{1,0:T(8,128)}, f32[4,48,128]{2,1,0:T(8,128)}, f32[16,512]{1,0:T(8,128)}) custom-call(s32[2,1024]{1,0:T(2,128)} %refs_0_.4, f32[16,512]{1,0:T(8,128)} %get-tuple-element.59.refs_1_, bf16[4,3,2048,128]{3,2,1,0:T(8,128)(2,1)} %get-tuple-element.60.refs_2_, ...), custom_call_target="tpu_custom_call" | custom-call | flops 20000000000 | bytes 30000000 | tf_op jit(solution)/shard_map/backward_scatter/pallas_call | solution.py:1204
  180.0 6.2 %update.1 = (f32[2048,512]{1,0:T(8,128)}, f32[3]{0:T(128)}, f32[16,1536]{1,0:T(8,128)}, f32[16,512]{1,0:T(8,128)}, f32[16,2048]{1,0:T(8,128)}, /*index=5*/f32[64...) custom-call(f32[144,512]{1,0:T(8,128)} %get-tuple-element.66.tot, ...), custom_call_target="tpu_custom_call" | custom-call | tf_op jit(solution)/shard_map/update/pallas_call | solution.py:1223
